TPU v7x, 256 devices: a whole 4x4x8 slice. The times are simulated.
256 devices in a mesh: expert: 16 (over x, y_hi, core), tensor: 8 (over z), dp: 2 (over y_lo).
Axes of the slice: x: 4, y: 4 (y_hi: 2, y_lo: 2; y = y_hi * 2 + y_lo), z: 8, core: 2. Of those that a mesh axis runs over, the one named last changes fastest.
Arguments:
- tokens: bfloat16 [8192, 3072], P(('expert', 'dp'), 'tensor'), may hold values from -6 to 6
- out_grad: bfloat16 [8192, 3072], P(('expert', 'dp'), 'tensor'), may hold values from -6 to 6
- gate_weight: bfloat16 [5376, 3072], P('expert', 'tensor'), may hold values from -0.109375 to 0.109375
- up_weight: bfloat16 [5376, 3072], P('expert', 'tensor'), may hold values from -0.109375 to 0.109375
- down_weight: bfloat16 [5376, 3072], P('expert', 'tensor'), may hold values from -0.078125 to 0.078125
- route_count: int32 [32], P(('expert', 'dp')), may hold values from 24 to 96, as said below
- route_index: int32 [3072], P(('expert', 'dp')), may hold values from 0 to 255, as said below
- route_gate: float32 [3072], P(('expert', 'dp')), may hold values from 0.1 to 1
Outputs:
- mixed: bfloat16 [8192, 3072], P(('expert', 'dp'), 'tensor')
- input_grad: bfloat16 [8192, 3072], P(('expert', 'dp'), 'tensor')
- grad_gate: float32 [5376, 3072], P('expert', ('tensor', 'dp'))
- grad_up: float32 [5376, 3072], P('expert', ('tensor', 'dp'))
- grad_down: float32 [5376, 3072], P('expert', ('tensor', 'dp'))
Inputs may be any that keep to these rules, and one draw needn't show every extreme that they name: `route_count`: one shard's count is exactly 96 and another's exactly 24. `route_index`: within one shard's 96 slots the token indices are distinct.
All inputs are finite; a program needn't handle non-finite values.
Results may differ from a plain program's by a relative error of at most 0.035.
Values may be sent and summed in bfloat16 or wider, within the bound.
No kernel may reach another device: no remote copies, remote signals or barrier semaphores. Data moves between devices by JAX's collectives and lax.ppermute only.
A program may use at most 64 MiB of HBM per device.

v0:
```python
import jax
import jax.numpy as jnp
from jax import lax
from jax.sharding import PartitionSpec as P


def passed_along(x, axis, by):
    size = lax.axis_size(axis)
    return lax.ppermute(x, axis, [(i, (i + by) % size) for i in range(size)])


def contract_features(left, right):
    return lax.dot_general(
        left, right, (((1,), (1,)), ((), ())), preferred_element_type=jnp.float32
    )


def contract_rows(left, right):
    return lax.dot_general(
        left, right, (((0,), (0,)), ((), ())), preferred_element_type=jnp.float32
    )


def partial_pre(rows_here, grads_here, weights):
    w_gate, w_up, w_down = weights
    return (
        contract_features(rows_here, w_gate),
        contract_features(rows_here, w_up),
        contract_features(grads_here, w_down),
    )


def finish_block(sums, weights):
    w_gate, w_up, w_down = weights
    gate_pre, up_pre, d_hidden = sums
    sigmoid_gate = jax.nn.sigmoid(gate_pre)
    activated = gate_pre * sigmoid_gate
    hidden = (activated * up_pre).astype(jnp.bfloat16)
    out_part = jnp.dot(hidden, w_down, preferred_element_type=jnp.float32)
    d_gate = (d_hidden * up_pre * sigmoid_gate * (1.0 + gate_pre * (1.0 - sigmoid_gate))).astype(
        jnp.bfloat16
    )
    d_up = (d_hidden * activated).astype(jnp.bfloat16)
    back_part = jnp.dot(d_gate, w_gate, preferred_element_type=jnp.float32) + jnp.dot(
        d_up, w_up, preferred_element_type=jnp.float32
    )
    return (hidden, d_gate, d_up, out_part, back_part)


def apply_slice(rows_here, grads_here, weights, accums, totals):
    parts = partial_pre(rows_here, grads_here, weights)
    sums = (
        lax.psum(parts[0].astype(jnp.bfloat16), "tensor").astype(jnp.float32),
        lax.psum(parts[1].astype(jnp.bfloat16), "tensor").astype(jnp.float32),
        lax.psum(parts[2].astype(jnp.bfloat16), "tensor").astype(jnp.float32),
    )
    hidden, d_gate, d_up, out_part, back_part = finish_block(sums, weights)
    new_gate = (accums[0].astype(jnp.float32) + contract_rows(d_gate, rows_here)).astype(
        jnp.bfloat16
    )
    new_up = (accums[1].astype(jnp.float32) + contract_rows(d_up, rows_here)).astype(jnp.bfloat16)
    new_down = (accums[2].astype(jnp.float32) + contract_rows(hidden, grads_here)).astype(
        jnp.bfloat16
    )
    return ((new_gate, new_up, new_down), (totals[0] + out_part, totals[1] + back_part))


def on_device(
    tokens, out_grad, gate_weight, up_weight, down_weight, route_count, route_index, route_gate
):
    capacity = route_index.shape[0]
    is_live = jnp.arange(capacity, dtype=jnp.int32) < route_count[0]
    route_weight = jnp.where(is_live, route_gate, 0.0)
    rows_here = jnp.take(tokens, route_index, axis=0)
    grads_here = (
        route_weight[:, None] * jnp.take(out_grad, route_index, axis=0).astype(jnp.float32)
    ).astype(jnp.bfloat16)
    width = tokens.shape[1]
    totals = (jnp.zeros((capacity, width), jnp.float32), jnp.zeros((capacity, width), jnp.float32))
    cycle_size = lax.axis_size("expert")
    weights = (gate_weight, up_weight, down_weight)
    empty = jnp.zeros(gate_weight.shape, jnp.bfloat16)

    def cycle_turn(step, state):
        slices, accums, sums = state
        accums, sums = apply_slice(rows_here, grads_here, slices, accums, sums)
        moved = passed_along(
            (slices[0], slices[1], slices[2], accums[0], accums[1], accums[2]), "expert", 1
        )
        return (tuple(moved[:3]), tuple(moved[3:]), sums)

    slices, accums, totals = lax.fori_loop(
        0, cycle_size - 1, cycle_turn, (weights, (empty, empty, empty), totals)
    )
    accums, totals = apply_slice(rows_here, grads_here, slices, accums, totals)
    accums = tuple(passed_along((accums[0], accums[1], accums[2]), "expert", 1))
    out_rows, back_rows = totals
    token_count = tokens.shape[0]
    mixed = (
        jnp.zeros((token_count, width), jnp.float32)
        .at[route_index]
        .add(route_weight[:, None] * out_rows)
    )
    input_grad = (
        jnp.zeros((token_count, width), jnp.float32)
        .at[route_index]
        .add(jnp.where(is_live[:, None], back_rows, 0.0))
    )
    grad_gate, grad_up, grad_down = (
        lax.psum_scatter(
            accums[0].astype(jnp.float32).astype(jnp.bfloat16),
            "dp",
            scatter_dimension=1,
            tiled=True,
        ).astype(jnp.float32),
        lax.psum_scatter(
            accums[1].astype(jnp.float32).astype(jnp.bfloat16),
            "dp",
            scatter_dimension=1,
            tiled=True,
        ).astype(jnp.float32),
        lax.psum_scatter(
            accums[2].astype(jnp.float32).astype(jnp.bfloat16),
            "dp",
            scatter_dimension=1,
            tiled=True,
        ).astype(jnp.float32),
    )
    return (
        mixed.astype(jnp.bfloat16),
        input_grad.astype(jnp.bfloat16),
        grad_gate,
        grad_up,
        grad_down,
    )


def solution(mesh):
    return jax.shard_map(
        on_device,
        mesh=mesh,
        in_specs=(
            P(("expert", "dp"), "tensor"),
            P(("expert", "dp"), "tensor"),
            P("expert", "tensor"),
            P("expert", "tensor"),
            P("expert", "tensor"),
            P(("expert", "dp")),
            P(("expert", "dp")),
            P(("expert", "dp")),
        ),
        out_specs=(
            P(("expert", "dp"), "tensor"),
            P(("expert", "dp"), "tensor"),
            P("expert", ("tensor", "dp")),
            P("expert", ("tensor", "dp")),
            P("expert", ("tensor", "dp")),
        ),
        check_vma=False,
    )
```

profile of v0, /device:TPU:1, one launch (start us, length us, event | category | flops | bytes accessed | tf_op | source)
XLA Modules:
  0.0 1513.1 jit_solution(10745646288844831721)
XLA Ops:
  13.2 1346.2 %while.25 = (s32[]{:T(128)}, bf16[336,384]{1,0:T(8,128)(2,1)S(1)}, bf16[336,384]{1,0:T(8,128)(2,1)S(1)}, bf16[336,384]{1,0:T(8,128)(2,1)S(1)}, bf16[336,384]{1,0...) while((s32[]{:T(128)}, bf16[336,384]{1,0:T(8,128)(2,1)S(1)}, ...), condition=%wide.region_4.6_spmd.clone, body=%wide.region_0.5_spmd.clone.sunk | while | flops 225944064 | bytes 15252980 | solution.py:92
  21.7 67.1 %all-reduce.9.cloned.1.call-done = (bf16[96,336]{1,0:T(8,128)(2,1)}, bf16[96,336]{1,0:T(8,128)(2,1)}, bf16[96,336]{1,0:T(8,128)(2,1)}) async-done(((bf16[96,336]{1,0:T(8,128)(2,1)}, bf16[96,336]{1,0:T(8,128)(2,1)}, bf16[96,336]{1,0:T(8,128)(2,1)}), (bf16[96,336]{1,0:T(8,128)(2,1)}, bf16[96,336]{1,0:T(8,128)(2,1)}, bf16[96,336]{1,0:T(8,128)(2,1)})) %all-reduce.9.cloned.1.call-update) | async-done | bytes 193552 | tf_op jit(solution)/shard_map/while/body/eval_jaxpr/psum | solution.py:54
  116.8 61.5 %all-reduce.9.cloned.1.call-done = (bf16[96,336]{1,0:T(8,128)(2,1)}, bf16[96,336]{1,0:T(8,128)(2,1)}, bf16[96,336]{1,0:T(8,128)(2,1)}) async-done(((bf16[96,336]{1,0:T(8,128)(2,1)}, bf16[96,336]{1,0:T(8,128)(2,1)}, bf16[96,336]{1,0:T(8,128)(2,1)}), (bf16[96,336]{1,0:T(8,128)(2,1)}, bf16[96,336]{1,0:T(8,128)(2,1)}, bf16[96,336]{1,0:T(8,128)(2,1)})) %all-reduce.9.cloned.1.call-update) | async-done | bytes 193552 | tf_op jit(solution)/shard_map/while/body/eval_jaxpr/psum | solution.py:54
  180.0 8.4 collective-permute-start.3
  206.4 61.5 %all-reduce.9.cloned.1.call-done = (bf16[96,336]{1,0:T(8,128)(2,1)}, bf16[96,336]{1,0:T(8,128)(2,1)}, bf16[96,336]{1,0:T(8,128)(2,1)}) async-done(((bf16[96,336]{1,0:T(8,128)(2,1)}, bf16[96,336]{1,0:T(8,128)(2,1)}, bf16[96,336]{1,0:T(8,128)(2,1)}), (bf16[96,336]{1,0:T(8,128)(2,1)}, bf16[96,336]{1,0:T(8,128)(2,1)}, bf16[96,336]{1,0:T(8,128)(2,1)})) %all-reduce.9.cloned.1.call-update) | async-done | bytes 193552 | tf_op jit(solution)/shard_map/while/body/eval_jaxpr/psum | solution.py:54
  296.0 61.2 %all-reduce.9.cloned.1.call-done = (bf16[96,336]{1,0:T(8,128)(2,1)}, bf16[96,336]{1,0:T(8,128)(2,1)}, bf16[96,336]{1,0:T(8,128)(2,1)}) async-done(((bf16[96,336]{1,0:T(8,128)(2,1)}, bf16[96,336]{1,0:T(8,128)(2,1)}, bf16[96,336]{1,0:T(8,128)(2,1)}), (bf16[96,336]{1,0:T(8,128)(2,1)}, bf16[96,336]{1,0:T(8,128)(2,1)}, bf16[96,336]{1,0:T(8,128)(2,1)})) %all-reduce.9.cloned.1.call-update) | async-done | bytes 193552 | tf_op jit(solution)/shard_map/while/body/eval_jaxpr/psum | solution.py:54
  385.2 61.1 %all-reduce.9.cloned.1.call-done = (bf16[96,336]{1,0:T(8,128)(2,1)}, bf16[96,336]{1,0:T(8,128)(2,1)}, bf16[96,336]{1,0:T(8,128)(2,1)}) async-done(((bf16[96,336]{1,0:T(8,128)(2,1)}, bf16[96,336]{1,0:T(8,128)(2,1)}, bf16[96,336]{1,0:T(8,128)(2,1)}), (bf16[96,336]{1,0:T(8,128)(2,1)}, bf16[96,336]{1,0:T(8,128)(2,1)}, bf16[96,336]{1,0:T(8,128)(2,1)})) %all-reduce.9.cloned.1.call-update) | async-done | bytes 193552 | tf_op jit(solution)/shard_map/while/body/eval_jaxpr/psum | solution.py:54
  474.4 61.1 %all-reduce.9.cloned.1.call-done = (bf16[96,336]{1,0:T(8,128)(2,1)}, bf16[96,336]{1,0:T(8,128)(2,1)}, bf16[96,336]{1,0:T(8,128)(2,1)}) async-done(((bf16[96,336]{1,0:T(8,128)(2,1)}, bf16[96,336]{1,0:T(8,128)(2,1)}, bf16[96,336]{1,0:T(8,128)(2,1)}), (bf16[96,336]{1,0:T(8,128)(2,1)}, bf16[96,336]{1,0:T(8,128)(2,1)}, bf16[96,336]{1,0:T(8,128)(2,1)})) %all-reduce.9.cloned.1.call-update) | async-done | bytes 193552 | tf_op jit(solution)/shard_map/while/body/eval_jaxpr/psum | solution.py:54
  563.7 61.5 %all-reduce.9.cloned.1.call-done = (bf16[96,336]{1,0:T(8,128)(2,1)}, bf16[96,336]{1,0:T(8,128)(2,1)}, bf16[96,336]{1,0:T(8,128)(2,1)}) async-done(((bf16[96,336]{1,0:T(8,128)(2,1)}, bf16[96,336]{1,0:T(8,128)(2,1)}, bf16[96,336]{1,0:T(8,128)(2,1)}), (bf16[96,336]{1,0:T(8,128)(2,1)}, bf16[96,336]{1,0:T(8,128)(2,1)}, bf16[96,336]{1,0:T(8,128)(2,1)})) %all-reduce.9.cloned.1.call-update) | async-done | bytes 193552 | tf_op jit(solution)/shard_map/while/body/eval_jaxpr/psum | solution.py:54
  653.3 61.5 %all-reduce.9.cloned.1.call-done = (bf16[96,336]{1,0:T(8,128)(2,1)}, bf16[96,336]{1,0:T(8,128)(2,1)}, bf16[96,336]{1,0:T(8,128)(2,1)}) async-done(((bf16[96,336]{1,0:T(8,128)(2,1)}, bf16[96,336]{1,0:T(8,128)(2,1)}, bf16[96,336]{1,0:T(8,128)(2,1)}), (bf16[96,336]{1,0:T(8,128)(2,1)}, bf16[96,336]{1,0:T(8,128)(2,1)}, bf16[96,336]{1,0:T(8,128)(2,1)})) %all-reduce.9.cloned.1.call-update) | async-done | bytes 193552 | tf_op jit(solution)/shard_map/while/body/eval_jaxpr/psum | solution.py:54
  742.9 61.5 %all-reduce.9.cloned.1.call-done = (bf16[96,336]{1,0:T(8,128)(2,1)}, bf16[96,336]{1,0:T(8,128)(2,1)}, bf16[96,336]{1,0:T(8,128)(2,1)}) async-done(((bf16[96,336]{1,0:T(8,128)(2,1)}, bf16[96,336]{1,0:T(8,128)(2,1)}, bf16[96,336]{1,0:T(8,128)(2,1)}), (bf16[96,336]{1,0:T(8,128)(2,1)}, bf16[96,336]{1,0:T(8,128)(2,1)}, bf16[96,336]{1,0:T(8,128)(2,1)})) %all-reduce.9.cloned.1.call-update) | async-done | bytes 193552 | tf_op jit(solution)/shard_map/while/body/eval_jaxpr/psum | solution.py:54
  832.4 61.2 %all-reduce.9.cloned.1.call-done = (bf16[96,336]{1,0:T(8,128)(2,1)}, bf16[96,336]{1,0:T(8,128)(2,1)}, bf16[96,336]{1,0:T(8,128)(2,1)}) async-done(((bf16[96,336]{1,0:T(8,128)(2,1)}, bf16[96,336]{1,0:T(8,128)(2,1)}, bf16[96,336]{1,0:T(8,128)(2,1)}), (bf16[96,336]{1,0:T(8,128)(2,1)}, bf16[96,336]{1,0:T(8,128)(2,1)}, bf16[96,336]{1,0:T(8,128)(2,1)})) %all-reduce.9.cloned.1.call-update) | async-done | bytes 193552 | tf_op jit(solution)/shard_map/while/body/eval_jaxpr/psum | solution.py:54
  895.3 8.4 collective-permute-start.3
  921.7 61.5 %all-reduce.9.cloned.1.call-done = (bf16[96,336]{1,0:T(8,128)(2,1)}, bf16[96,336]{1,0:T(8,128)(2,1)}, bf16[96,336]{1,0:T(8,128)(2,1)}) async-done(((bf16[96,336]{1,0:T(8,128)(2,1)}, bf16[96,336]{1,0:T(8,128)(2,1)}, bf16[96,336]{1,0:T(8,128)(2,1)}), (bf16[96,336]{1,0:T(8,128)(2,1)}, bf16[96,336]{1,0:T(8,128)(2,1)}, bf16[96,336]{1,0:T(8,128)(2,1)})) %all-reduce.9.cloned.1.call-update) | async-done | bytes 193552 | tf_op jit(solution)/shard_map/while/body/eval_jaxpr/psum | solution.py:54
  1011.3 61.2 %all-reduce.9.cloned.1.call-done = (bf16[96,336]{1,0:T(8,128)(2,1)}, bf16[96,336]{1,0:T(8,128)(2,1)}, bf16[96,336]{1,0:T(8,128)(2,1)}) async-done(((bf16[96,336]{1,0:T(8,128)(2,1)}, bf16[96,336]{1,0:T(8,128)(2,1)}, bf16[96,336]{1,0:T(8,128)(2,1)}), (bf16[96,336]{1,0:T(8,128)(2,1)}, bf16[96,336]{1,0:T(8,128)(2,1)}, bf16[96,336]{1,0:T(8,128)(2,1)})) %all-reduce.9.cloned.1.call-update) | async-done | bytes 193552 | tf_op jit(solution)/shard_map/while/body/eval_jaxpr/psum | solution.py:54
  1074.2 8.4 collective-permute-start.3
  1100.6 61.4 %all-reduce.9.cloned.1.call-done = (bf16[96,336]{1,0:T(8,128)(2,1)}, bf16[96,336]{1,0:T(8,128)(2,1)}, bf16[96,336]{1,0:T(8,128)(2,1)}) async-done(((bf16[96,336]{1,0:T(8,128)(2,1)}, bf16[96,336]{1,0:T(8,128)(2,1)}, bf16[96,336]{1,0:T(8,128)(2,1)}), (bf16[96,336]{1,0:T(8,128)(2,1)}, bf16[96,336]{1,0:T(8,128)(2,1)}, bf16[96,336]{1,0:T(8,128)(2,1)})) %all-reduce.9.cloned.1.call-update) | async-done | bytes 193552 | tf_op jit(solution)/shard_map/while/body/eval_jaxpr/psum | solution.py:54
  1163.7 8.4 collective-permute-start.3
  1190.1 61.2 %all-reduce.9.cloned.1.call-done = (bf16[96,336]{1,0:T(8,128)(2,1)}, bf16[96,336]{1,0:T(8,128)(2,1)}, bf16[96,336]{1,0:T(8,128)(2,1)}) async-done(((bf16[96,336]{1,0:T(8,128)(2,1)}, bf16[96,336]{1,0:T(8,128)(2,1)}, bf16[96,336]{1,0:T(8,128)(2,1)}), (bf16[96,336]{1,0:T(8,128)(2,1)}, bf16[96,336]{1,0:T(8,128)(2,1)}, bf16[96,336]{1,0:T(8,128)(2,1)})) %all-reduce.9.cloned.1.call-update) | async-done | bytes 193552 | tf_op jit(solution)/shard_map/while/body/eval_jaxpr/psum | solution.py:54
  1252.9 8.4 collective-permute-start.3
  1279.3 61.1 %all-reduce.9.cloned.1.call-done = (bf16[96,336]{1,0:T(8,128)(2,1)}, bf16[96,336]{1,0:T(8,128)(2,1)}, bf16[96,336]{1,0:T(8,128)(2,1)}) async-done(((bf16[96,336]{1,0:T(8,128)(2,1)}, bf16[96,336]{1,0:T(8,128)(2,1)}, bf16[96,336]{1,0:T(8,128)(2,1)}), (bf16[96,336]{1,0:T(8,128)(2,1)}, bf16[96,336]{1,0:T(8,128)(2,1)}, bf16[96,336]{1,0:T(8,128)(2,1)})) %all-reduce.9.cloned.1.call-update) | async-done | bytes 193552 | tf_op jit(solution)/shard_map/while/body/eval_jaxpr/psum | solution.py:54
  1362.0 67.6 %all-reduce.7.cloned.1.call-done = (bf16[96,336]{1,0:T(8,128)(2,1)}, bf16[96,336]{1,0:T(8,128)(2,1)}, bf16[96,336]{1,0:T(8,128)(2,1)}) async-done(((bf16[96,336]{1,0:T(8,128)(2,1)}, bf16[96,336]{1,0:T(8,128)(2,1)}, bf16[96,336]{1,0:T(8,128)(2,1)}), (bf16[96,336]{1,0:T(8,128)(2,1)}, bf16[96,336]{1,0:T(8,128)(2,1)}, bf16[96,336]{1,0:T(8,128)(2,1)})) %all-reduce.7.cloned.1.call-update) | async-done | bytes 193552 | tf_op jit(solution)/shard_map/psum | solution.py:54
  1468.7 14.5 reduce-scatter.12.cloned.1.call-done
  1485.1 18.8 %reduce-scatter.14.cloned.1.call-done = bf16[192,336]{1,0:T(8,128)(2,1)} async-done(((bf16[384,336]{1,0:T(8,128)(2,1)}), bf16[192,336]{1,0:T(8,128)(2,1)}) %reduce-scatter.14.cloned.1.call-update) | async-done | bytes 129040
  (562 shorter events, 426.4 us)
Async XLA Ops:
  15.9 83.6 %collective-permute-start = (bf16[336,384]{1,0:T(8,128)(2,1)S(1)}, bf16[336,384]{1,0:T(8,128)(2,1)S(1)}, u32[]{:S(2)}, u32[]{:S(2)}) collective-permute-start(bf16[336,384]{1,0:T(8,128)(2,1)S(1)} %copy.41), channel_id=1, source_target_pairs={{0,16},{16,32},{32,48},{48,64},{64,80},{80,96},{96,112},{112,128},... | collective-permute-start | bytes 774152 | tf_op jit(solution)/shard_map/while/body/eval_jaxpr/ppermute | solution.py:9
  20.3 81.2 %collective-permute-start.1 = (bf16[336,384]{1,0:T(8,128)(2,1)S(1)}, bf16[336,384]{1,0:T(8,128)(2,1)S(1)}, u32[]{:S(2)}, u32[]{:S(2)}) collective-permute-start(bf16[336,384]{1,0:T(8,128)(2,1)S(1)} %copy.42), channel_id=1, source_target_pairs={{0,16},{16,32},{32,48},{48,64},{64,80},{80,96},{96,112},{112,128},... | collective-permute-start | bytes 774152 | tf_op jit(solution)/shard_map/while/body/eval_jaxpr/ppermute | solution.py:9
  20.3 81.1 %collective-permute-start.2 = (bf16[336,384]{1,0:T(8,128)(2,1)S(1)}, bf16[336,384]{1,0:T(8,128)(2,1)S(1)}, u32[]{:S(2)}, u32[]{:S(2)}) collective-permute-start(bf16[336,384]{1,0:T(8,128)(2,1)S(1)} %copy.43), channel_id=1, source_target_pairs={{0,16},{16,32},{32,48},{48,64},{64,80},{80,96},{96,112},{112,128},... | collective-permute-start | bytes 774152 | tf_op jit(solution)/shard_map/while/body/eval_jaxpr/ppermute | solution.py:9
  110.3 78.7 %collective-permute-start = (bf16[336,384]{1,0:T(8,128)(2,1)S(1)}, bf16[336,384]{1,0:T(8,128)(2,1)S(1)}, u32[]{:S(2)}, u32[]{:S(2)}) collective-permute-start(bf16[336,384]{1,0:T(8,128)(2,1)S(1)} %copy.41), channel_id=1, source_target_pairs={{0,16},{16,32},{32,48},{48,64},{64,80},{80,96},{96,112},{112,128},... | collective-permute-start | bytes 774152 | tf_op jit(solution)/shard_map/while/body/eval_jaxpr/ppermute | solution.py:9
  114.4 76.6 %collective-permute-start.1 = (bf16[336,384]{1,0:T(8,128)(2,1)S(1)}, bf16[336,384]{1,0:T(8,128)(2,1)S(1)}, u32[]{:S(2)}, u32[]{:S(2)}) collective-permute-start(bf16[336,384]{1,0:T(8,128)(2,1)S(1)} %copy.42), channel_id=1, source_target_pairs={{0,16},{16,32},{32,48},{48,64},{64,80},{80,96},{96,112},{112,128},... | collective-permute-start | bytes 774152 | tf_op jit(solution)/shard_map/while/body/eval_jaxpr/ppermute | solution.py:9
  199.9 78.7 %collective-permute-start = (bf16[336,384]{1,0:T(8,128)(2,1)S(1)}, bf16[336,384]{1,0:T(8,128)(2,1)S(1)}, u32[]{:S(2)}, u32[]{:S(2)}) collective-permute-start(bf16[336,384]{1,0:T(8,128)(2,1)S(1)} %copy.41), channel_id=1, source_target_pairs={{0,16},{16,32},{32,48},{48,64},{64,80},{80,96},{96,112},{112,128},... | collective-permute-start | bytes 774152 | tf_op jit(solution)/shard_map/while/body/eval_jaxpr/ppermute | solution.py:9
  203.9 76.7 %collective-permute-start.1 = (bf16[336,384]{1,0:T(8,128)(2,1)S(1)}, bf16[336,384]{1,0:T(8,128)(2,1)S(1)}, u32[]{:S(2)}, u32[]{:S(2)}) collective-permute-start(bf16[336,384]{1,0:T(8,128)(2,1)S(1)} %copy.42), channel_id=1, source_target_pairs={{0,16},{16,32},{32,48},{48,64},{64,80},{80,96},{96,112},{112,128},... | collective-permute-start | bytes 774152 | tf_op jit(solution)/shard_map/while/body/eval_jaxpr/ppermute | solution.py:9
  289.5 78.4 %collective-permute-start = (bf16[336,384]{1,0:T(8,128)(2,1)S(1)}, bf16[336,384]{1,0:T(8,128)(2,1)S(1)}, u32[]{:S(2)}, u32[]{:S(2)}) collective-permute-start(bf16[336,384]{1,0:T(8,128)(2,1)S(1)} %copy.41), channel_id=1, source_target_pairs={{0,16},{16,32},{32,48},{48,64},{64,80},{80,96},{96,112},{112,128},... | collective-permute-start | bytes 774152 | tf_op jit(solution)/shard_map/while/body/eval_jaxpr/ppermute | solution.py:9
  378.8 78.3 %collective-permute-start = (bf16[336,384]{1,0:T(8,128)(2,1)S(1)}, bf16[336,384]{1,0:T(8,128)(2,1)S(1)}, u32[]{:S(2)}, u32[]{:S(2)}) collective-permute-start(bf16[336,384]{1,0:T(8,128)(2,1)S(1)} %copy.41), channel_id=1, source_target_pairs={{0,16},{16,32},{32,48},{48,64},{64,80},{80,96},{96,112},{112,128},... | collective-permute-start | bytes 774152 | tf_op jit(solution)/shard_map/while/body/eval_jaxpr/ppermute | solution.py:9
  467.9 78.4 %collective-permute-start = (bf16[336,384]{1,0:T(8,128)(2,1)S(1)}, bf16[336,384]{1,0:T(8,128)(2,1)S(1)}, u32[]{:S(2)}, u32[]{:S(2)}) collective-permute-start(bf16[336,384]{1,0:T(8,128)(2,1)S(1)} %copy.41), channel_id=1, source_target_pairs={{0,16},{16,32},{32,48},{48,64},{64,80},{80,96},{96,112},{112,128},... | collective-permute-start | bytes 774152 | tf_op jit(solution)/shard_map/while/body/eval_jaxpr/ppermute | solution.py:9
  557.2 78.7 %collective-permute-start = (bf16[336,384]{1,0:T(8,128)(2,1)S(1)}, bf16[336,384]{1,0:T(8,128)(2,1)S(1)}, u32[]{:S(2)}, u32[]{:S(2)}) collective-permute-start(bf16[336,384]{1,0:T(8,128)(2,1)S(1)} %copy.41), channel_id=1, source_target_pairs={{0,16},{16,32},{32,48},{48,64},{64,80},{80,96},{96,112},{112,128},... | collective-permute-start | bytes 774152 | tf_op jit(solution)/shard_map/while/body/eval_jaxpr/ppermute | solution.py:9
  561.2 76.7 %collective-permute-start.1 = (bf16[336,384]{1,0:T(8,128)(2,1)S(1)}, bf16[336,384]{1,0:T(8,128)(2,1)S(1)}, u32[]{:S(2)}, u32[]{:S(2)}) collective-permute-start(bf16[336,384]{1,0:T(8,128)(2,1)S(1)} %copy.42), channel_id=1, source_target_pairs={{0,16},{16,32},{32,48},{48,64},{64,80},{80,96},{96,112},{112,128},... | collective-permute-start | bytes 774152 | tf_op jit(solution)/shard_map/while/body/eval_jaxpr/ppermute | solution.py:9
  646.8 78.7 %collective-permute-start = (bf16[336,384]{1,0:T(8,128)(2,1)S(1)}, bf16[336,384]{1,0:T(8,128)(2,1)S(1)}, u32[]{:S(2)}, u32[]{:S(2)}) collective-permute-start(bf16[336,384]{1,0:T(8,128)(2,1)S(1)} %copy.41), channel_id=1, source_target_pairs={{0,16},{16,32},{32,48},{48,64},{64,80},{80,96},{96,112},{112,128},... | collective-permute-start | bytes 774152 | tf_op jit(solution)/shard_map/while/body/eval_jaxpr/ppermute | solution.py:9
  650.8 76.7 %collective-permute-start.1 = (bf16[336,384]{1,0:T(8,128)(2,1)S(1)}, bf16[336,384]{1,0:T(8,128)(2,1)S(1)}, u32[]{:S(2)}, u32[]{:S(2)}) collective-permute-start(bf16[336,384]{1,0:T(8,128)(2,1)S(1)} %copy.42), channel_id=1, source_target_pairs={{0,16},{16,32},{32,48},{48,64},{64,80},{80,96},{96,112},{112,128},... | collective-permute-start | bytes 774152 | tf_op jit(solution)/shard_map/while/body/eval_jaxpr/ppermute | solution.py:9
  736.3 78.7 %collective-permute-start = (bf16[336,384]{1,0:T(8,128)(2,1)S(1)}, bf16[336,384]{1,0:T(8,128)(2,1)S(1)}, u32[]{:S(2)}, u32[]{:S(2)}) collective-permute-start(bf16[336,384]{1,0:T(8,128)(2,1)S(1)} %copy.41), channel_id=1, source_target_pairs={{0,16},{16,32},{32,48},{48,64},{64,80},{80,96},{96,112},{112,128},... | collective-permute-start | bytes 774152 | tf_op jit(solution)/shard_map/while/body/eval_jaxpr/ppermute | solution.py:9
  740.4 76.7 %collective-permute-start.1 = (bf16[336,384]{1,0:T(8,128)(2,1)S(1)}, bf16[336,384]{1,0:T(8,128)(2,1)S(1)}, u32[]{:S(2)}, u32[]{:S(2)}) collective-permute-start(bf16[336,384]{1,0:T(8,128)(2,1)S(1)} %copy.42), channel_id=1, source_target_pairs={{0,16},{16,32},{32,48},{48,64},{64,80},{80,96},{96,112},{112,128},... | collective-permute-start | bytes 774152 | tf_op jit(solution)/shard_map/while/body/eval_jaxpr/ppermute | solution.py:9
  825.9 78.4 %collective-permute-start = (bf16[336,384]{1,0:T(8,128)(2,1)S(1)}, bf16[336,384]{1,0:T(8,128)(2,1)S(1)}, u32[]{:S(2)}, u32[]{:S(2)}) collective-permute-start(bf16[336,384]{1,0:T(8,128)(2,1)S(1)} %copy.41), channel_id=1, source_target_pairs={{0,16},{16,32},{32,48},{48,64},{64,80},{80,96},{96,112},{112,128},... | collective-permute-start | bytes 774152 | tf_op jit(solution)/shard_map/while/body/eval_jaxpr/ppermute | solution.py:9
  915.2 78.7 %collective-permute-start = (bf16[336,384]{1,0:T(8,128)(2,1)S(1)}, bf16[336,384]{1,0:T(8,128)(2,1)S(1)}, u32[]{:S(2)}, u32[]{:S(2)}) collective-permute-start(bf16[336,384]{1,0:T(8,128)(2,1)S(1)} %copy.41), channel_id=1, source_target_pairs={{0,16},{16,32},{32,48},{48,64},{64,80},{80,96},{96,112},{112,128},... | collective-permute-start | bytes 774152 | tf_op jit(solution)/shard_map/while/body/eval_jaxpr/ppermute | solution.py:9
  919.3 76.7 %collective-permute-start.1 = (bf16[336,384]{1,0:T(8,128)(2,1)S(1)}, bf16[336,384]{1,0:T(8,128)(2,1)S(1)}, u32[]{:S(2)}, u32[]{:S(2)}) collective-permute-start(bf16[336,384]{1,0:T(8,128)(2,1)S(1)} %copy.42), channel_id=1, source_target_pairs={{0,16},{16,32},{32,48},{48,64},{64,80},{80,96},{96,112},{112,128},... | collective-permute-start | bytes 774152 | tf_op jit(solution)/shard_map/while/body/eval_jaxpr/ppermute | solution.py:9
  1004.8 78.4 %collective-permute-start = (bf16[336,384]{1,0:T(8,128)(2,1)S(1)}, bf16[336,384]{1,0:T(8,128)(2,1)S(1)}, u32[]{:S(2)}, u32[]{:S(2)}) collective-permute-start(bf16[336,384]{1,0:T(8,128)(2,1)S(1)} %copy.41), channel_id=1, source_target_pairs={{0,16},{16,32},{32,48},{48,64},{64,80},{80,96},{96,112},{112,128},... | collective-permute-start | bytes 774152 | tf_op jit(solution)/shard_map/while/body/eval_jaxpr/ppermute | solution.py:9
  1094.1 78.7 %collective-permute-start = (bf16[336,384]{1,0:T(8,128)(2,1)S(1)}, bf16[336,384]{1,0:T(8,128)(2,1)S(1)}, u32[]{:S(2)}, u32[]{:S(2)}) collective-permute-start(bf16[336,384]{1,0:T(8,128)(2,1)S(1)} %copy.41), channel_id=1, source_target_pairs={{0,16},{16,32},{32,48},{48,64},{64,80},{80,96},{96,112},{112,128},... | collective-permute-start | bytes 774152 | tf_op jit(solution)/shard_map/while/body/eval_jaxpr/ppermute | solution.py:9
  1183.6 78.4 %collective-permute-start = (bf16[336,384]{1,0:T(8,128)(2,1)S(1)}, bf16[336,384]{1,0:T(8,128)(2,1)S(1)}, u32[]{:S(2)}, u32[]{:S(2)}) collective-permute-start(bf16[336,384]{1,0:T(8,128)(2,1)S(1)} %copy.41), channel_id=1, source_target_pairs={{0,16},{16,32},{32,48},{48,64},{64,80},{80,96},{96,112},{112,128},... | collective-permute-start | bytes 774152 | tf_op jit(solution)/shard_map/while/body/eval_jaxpr/ppermute | solution.py:9
  1272.9 78.3 %collective-permute-start = (bf16[336,384]{1,0:T(8,128)(2,1)S(1)}, bf16[336,384]{1,0:T(8,128)(2,1)S(1)}, u32[]{:S(2)}, u32[]{:S(2)}) collective-permute-start(bf16[336,384]{1,0:T(8,128)(2,1)S(1)} %copy.41), channel_id=1, source_target_pairs={{0,16},{16,32},{32,48},{48,64},{64,80},{80,96},{96,112},{112,128},... | collective-permute-start | bytes 774152 | tf_op jit(solution)/shard_map/while/body/eval_jaxpr/ppermute | solution.py:9
  1361.9 104.9 %reduce-scatter.10.cloned.1.call-start = ((), (), s32[]{:S(2)}) async-start(), calls=%async_computation.3 | async-start | bytes 442368
  (143 other events, 3492.6 us)
Sparse Core Ops, SparseCore 0:
  17.3 71.3 all-reduce.8
  111.8 66.4 all-reduce.8
  201.3 66.5 all-reduce.8
  290.6 66.5 all-reduce.8
  379.9 66.4 all-reduce.8
  469.1 66.4 all-reduce.8
  558.6 66.5 all-reduce.8
  648.2 66.5 all-reduce.8
  737.8 66.5 all-reduce.8
  827.0 66.5 all-reduce.8
  916.6 66.5 all-reduce.8
  1005.9 66.5 all-reduce.8
  1095.5 66.4 all-reduce.8
  1184.7 66.5 all-reduce.8
  1274.0 66.4 all-reduce.8
Sparse Core Ops, SparseCore 1:
  1362.9 66.5 all-reduce.6
  1443.5 15.7 reduce-scatter.9
  1462.4 20.7 reduce-scatter.11
  1485.9 18.0 reduce-scatter.13
where the time goes:
time: 1510 us
  waiting for transfers between devices  1130 us (75%)
  starting transfers between devices  264 us (17%)
  matrix products  65 us (4%)
  other arithmetic  21.2 us (1%)
  between operations  16.3 us (1%)
  local copies, waits for them, and re-layouts  15.6 us (1%)
    psum x16, waiting for transfers between devices, apply_slice(): lax.psum(parts[1].astype(jnp.bfloat16), 'tensor').astype(jnp.float32)  993 us
    ppermute x93, starting transfers between devices, passed_along(): return lax.ppermute(x, axis, [(i, (i + by) % size) for i in range(size)])  264 us
    ppermute x93, waiting for transfers between devices, passed_along(): return lax.ppermute(x, axis, [(i, (i + by) % size) for i in range(size)])  102 us
    dot_general x48, matrix products, contract_features(): lax.dot_general(left, right, (((1,), (1,)), ((), ())), preferred_element_...  40.8 us
    unnamed x7, waiting for transfers between devices  33.4 us
  transfers between devices with their start and end apart: 112, of which 66 were waited for; matrix products, arithmetic and copies ran while one was open for 3% of the time, Pallas kernels for 0%

commit v1 on v0

v1 whole, which is shorter than its diff:
```python
import jax
import jax.numpy as jnp
from jax import lax
from jax.sharding import PartitionSpec as P

BF16 = jnp.bfloat16
F32 = jnp.float32


def dot(left, right, left_dim, right_dim):
    return lax.dot_general(
        left, right, (((left_dim,), (right_dim,)), ((), ())), preferred_element_type=F32
    )


def on_device(
    tokens, out_grad, gate_weight, up_weight, down_weight, route_count, route_index, route_gate
):
    capacity = route_index.shape[0]
    token_count, width = tokens.shape
    block = gate_weight.shape[0]
    is_live = jnp.arange(capacity, dtype=jnp.int32) < route_count[0]
    route_weight = jnp.where(is_live, route_gate, 0.0)
    pick = (
        route_index[:, None] == jnp.arange(token_count, dtype=jnp.int32)[None, :]
    ).astype(BF16)
    rows_here = dot(pick, tokens, 1, 0).astype(BF16)
    grads_here = (route_weight[:, None] * dot(pick, out_grad, 1, 0)).astype(BF16)

    gathered = lax.all_gather(
        jnp.concatenate([rows_here, grads_here], axis=1), "expert", axis=0, tiled=True
    )
    rows, grads = gathered[:, :width], gathered[:, width:]

    pre = jnp.concatenate(
        [
            dot(rows, gate_weight, 1, 1).astype(BF16),
            dot(rows, up_weight, 1, 1).astype(BF16),
            dot(grads, down_weight, 1, 1).astype(BF16),
        ],
        axis=1,
    )
    sums = lax.psum_scatter(pre, "tensor", scatter_dimension=0, tiled=True).astype(F32)
    gate_pre, up_pre, d_hidden = sums[:, :block], sums[:, block : 2 * block], sums[:, 2 * block :]
    sigmoid_gate = jax.nn.sigmoid(gate_pre)
    activated = gate_pre * sigmoid_gate
    hidden = (activated * up_pre).astype(BF16)
    d_gate = (d_hidden * up_pre * sigmoid_gate * (1.0 + gate_pre * (1.0 - sigmoid_gate))).astype(
        BF16
    )
    d_up = (d_hidden * activated).astype(BF16)
    acts = lax.all_gather(
        jnp.concatenate([hidden, d_gate, d_up], axis=1), "tensor", axis=0, tiled=True
    )
    hidden, d_gate, d_up = acts[:, :block], acts[:, block : 2 * block], acts[:, 2 * block :]

    out_part = dot(hidden, down_weight, 1, 0)
    back_part = dot(d_gate, gate_weight, 1, 0) + dot(d_up, up_weight, 1, 0)
    mine = lax.psum_scatter(
        jnp.concatenate([out_part.astype(BF16), back_part.astype(BF16)], axis=1),
        "expert",
        scatter_dimension=0,
        tiled=True,
    ).astype(F32)
    out_rows = (route_weight[:, None] * mine[:, :width]).astype(BF16)
    back_rows = jnp.where(is_live[:, None], mine[:, width:], 0.0).astype(BF16)
    mixed = dot(pick, out_rows, 0, 0).astype(BF16)
    input_grad = dot(pick, back_rows, 0, 0).astype(BF16)

    grads_w = jnp.concatenate(
        [dot(d_gate, rows, 0, 0), dot(d_up, rows, 0, 0), dot(hidden, grads, 0, 0)], axis=0
    ).astype(BF16)
    half = width // 2
    first = lax.axis_index("dp") == 0
    low, high = grads_w[:, :half], grads_w[:, half:]
    got = lax.ppermute(jnp.where(first, high, low), "dp", [(0, 1), (1, 0)])
    total = jnp.where(first, low, high).astype(F32) + got.astype(F32)
    return (
        mixed,
        input_grad,
        total[:block],
        total[block : 2 * block],
        total[2 * block :],
    )


def solution(mesh):
    return jax.shard_map(
        on_device,
        mesh=mesh,
        in_specs=(
            P(("expert", "dp"), "tensor"),
            P(("expert", "dp"), "tensor"),
            P("expert", "tensor"),
            P("expert", "tensor"),
            P("expert", "tensor"),
            P(("expert", "dp")),
            P(("expert", "dp")),
            P(("expert", "dp")),
        ),
        out_specs=(
            P(("expert", "dp"), "tensor"),
            P(("expert", "dp"), "tensor"),
            P("expert", ("tensor", "dp")),
            P("expert", ("tensor", "dp")),
            P("expert", ("tensor", "dp")),
        ),
        check_vma=False,
    )
```

time: 1510 us -> 264 us (0.17)
  waiting for transfers between devices: 1130 us -> 216 us
  starting transfers between devices: 264 us -> 1.45 us
  matrix products: 65 us -> 17.8 us
  other arithmetic: 21.2 us -> 5.05 us
    psum x16 -> x0, waiting for transfers between devices: 993 us -> none  [apply_slice(): lax.psum(parts[1].astype(jnp.bfloat16), 'tensor').astype(jnp.float32)]
    ppermute x93 -> x1, starting transfers between devices: 264 us -> 1.28 us  [on_device(): got = lax.ppermute(jnp.where(first, high, low), 'dp', [(0, 1), (1, 0)])]
    all_gather x0 -> x2, waiting for transfers between devices: none -> 106 us  [the longest x1 58.8 us: on_device(): lax.all_gather(jnp.concatenate([rows_here, grads_here], axis=1), 'expert'...]
    ppermute x93 -> x1, waiting for transfers between devices: 102 us -> 11.2 us  [on_device(): got = lax.ppermute(jnp.where(first, high, low), 'dp', [(0, 1), (1, 0)])]
    reduce_scatter x0 -> x1, waiting for transfers between devices: none -> 56.9 us  [on_device(): lax.psum_scatter(jnp.concatenate([out_part.astype(BF16), back_part.astype...]
    dot_general x144 -> x13, matrix products: 65 us -> 17.8 us  [dot(): lax.dot_general(left, right, (((left_dim,), (right_dim,)), ((), ())), pre...]
    convert_element_type x19 -> x3, other arithmetic: 18.6 us -> 1.21 us  [the longest x1 0.93 us: on_device(): mine = lax.psum_scatter(jnp.concatenate([out_part.astype(BF16), back_part...]
    unnamed x7 -> x5, waiting for transfers between devices: 33.4 us -> 42.7 us
  transfers between devices with their start and end apart: 112 -> 5, of which waited for: 66 -> 5; matrix products, arithmetic and copies ran while one was open for 3% -> 3% of each run, Pallas kernels for 0% -> 0%
where the time goes in v1:
time: 264 us; the launch traced here: 263 us
  waiting for transfers between devices  216 us (82%)
  matrix products  17.8 us (7%)
  between operations  14.8 us (6%)
  local copies, waits for them, and re-layouts  7.75 us (3%)
  other arithmetic  5.05 us (2%)
    all_gather x1, waiting for transfers between devices, on_device(): lax.all_gather(jnp.concatenate([rows_here, grads_here], axis=1), 'expert'...  58.8 us
    reduce_scatter x1, waiting for transfers between devices, on_device(): lax.psum_scatter(jnp.concatenate([out_part.astype(BF16), back_part.astype...  56.9 us
    all_gather x1, waiting for transfers between devices, on_device(): lax.all_gather(jnp.concatenate([hidden, d_gate, d_up], axis=1), 'tensor',...  46.9 us
    unnamed x5, waiting for transfers between devices  42.7 us
    dot_general x13, matrix products, dot(): lax.dot_general(left, right, (((left_dim,), (right_dim,)), ((), ())), pre...  17.8 us
    ppermute x1, waiting for transfers between devices, on_device(): got = lax.ppermute(jnp.where(first, high, low), 'dp', [(0, 1), (1, 0)])  11.2 us
    unnamed x19, local copies, waits for them, and re-layouts  6.73 us
  transfers between devices with their start and end apart: 5, of which 5 were waited for; matrix products, arithmetic and copies ran while one was open for 3% of the time, Pallas kernels for 0%

profile of v1, /device:TPU:1, one launch (start us, length us, event | category | flops | bytes accessed | tf_op | source)
XLA Modules:
  0.0 263.2 jit_solution(13116408395989421982)
XLA Ops:
  8.7 1.2 convolution_convert_fusion.9
  9.8 1.2 fusion.1
  11.7 58.8 %all-gather.3.cloned.1.call-done = bf16[1536,768]{1,0:T(8,128)(2,1)} async-done(((bf16[96,768]{1,0:T(8,128)(2,1)}), bf16[1536,768]{1,0:T(8,128)(2,1)}) %all-gather.3.cloned.1.call-update) | async-done | bytes 2359312 | tf_op jit(solution)/shard_map/all_gather | solution.py:30
  70.6 2.2 convolution_convert_fusion.1
  74.5 2.9 %copy.29 = bf16[1536,1008]{1,0:T(8,128)(2,1)} copy(bf16[1536,1008]{0,1:T(8,128)(2,1)S(1)} %pad_maximum_fusion) | data formatting | bytes 6193152
  77.5 42.7 %reduce-scatter.7.cloned.1.call-done = bf16[192,1008]{1,0:T(8,128)(2,1)} async-done(((bf16[1536,1008]{1,0:T(8,128)(2,1)}), bf16[192,1008]{1,0:T(8,128)(2,1)}) %reduce-scatter.7.cloned.1.call-update) | async-done | bytes 387088
  120.1 1.2 copy.30
  121.7 0.9 copy.19
  122.7 46.9 %all-gather.5.cloned.1.call-done = bf16[1536,1008]{1,0:T(8,128)(2,1)} async-done(((bf16[192,1008]{1,0:T(8,128)(2,1)}), bf16[1536,1008]{1,0:T(8,128)(2,1)}) %all-gather.5.cloned.1.call-update) | async-done | bytes 3096592 | tf_op jit(solution)/shard_map/all_gather | solution.py:52
  169.6 2.5 fusion.5
  172.1 1.9 convolution_convert_fusion
  174.0 1.0 fusion
  175.0 1.6 pad_maximum_fusion.1
  176.7 2.2 convolution_convert_fusion.4
  178.8 1.2 convolution_convert_fusion.5
  180.0 1.2 convolution_convert_fusion.6
  181.5 1.3 collective-permute-start
  182.7 11.2 %collective-permute-done = bf16[1008,192]{1,0:T(8,128)(2,1)S(1)} collective-permute-done((bf16[1008,192]{1,0:T(8,128)(2,1)S(1)}, bf16[1008,192]{1,0:T(8,128)(2,1)S(1)}, u32[]{:S(2)}, u32[]{:S(2)}) %collective-permute-start) | collective-permute-done | bytes 387104 | tf_op jit(solution)/shard_map/ppermute | solution.py:76
  194.3 0.9 copy.23
  195.2 0.9 copy.24
  196.9 56.9 %reduce-scatter.5.cloned.1.call-done = bf16[96,768]{1,0:T(8,128)(2,1)} async-done(((bf16[1536,768]{1,0:T(8,128)(2,1)}), bf16[96,768]{1,0:T(8,128)(2,1)}) %reduce-scatter.5.cloned.1.call-update) | async-done | bytes 147472 | tf_op jit(solution)/shard_map/reduce_scatter | solution.py:59
  253.7 0.9 convert_element_type.67
  254.7 1.0 convolution_convert_fusion.8
  255.7 1.0 convolution_convert_fusion.7
  (36 shorter events, 5.2 us)
Async XLA Ops:
  7.2 66.4 %copy-start = (bf16[336,384]{1,0:T(8,128)(2,1)S(1)}, bf16[336,384]{1,0:T(8,128)(2,1)}, u32[]{:S(2)}) copy-start(bf16[336,384]{1,0:T(8,128)(2,1)} %param.10) | copy-start | bytes 774148
  7.2 65.6 %copy-start.2 = (bf16[336,384]{1,0:T(8,128)(2,1)S(1)}, bf16[336,384]{1,0:T(8,128)(2,1)}, u32[]{:S(2)}) copy-start(bf16[336,384]{1,0:T(8,128)(2,1)} %param.11) | copy-start | bytes 774148
  7.2 63.4 %all-gather.3.cloned.1.call-start = ((), (), s32[]{:S(2)}) async-start(), calls=%async_computation.2 | async-start | bytes 2506752 | tf_op jit(solution)/shard_map/all_gather | solution.py:30
  11.7 108.4 %reduce-scatter.7.cloned.1.call-start = ((), (), s32[]{:S(2)}) async-start(), calls=%async_computation.5 | async-start | bytes 3538944
  70.6 2.2 copy-start.5
  77.4 92.2 %all-gather.5.cloned.1.call-start = ((), (), s32[]{:S(2)}) async-start(), calls=%async_computation.3 | async-start | bytes 3538944 | tf_op jit(solution)/shard_map/all_gather | solution.py:52
  122.7 131.1 %reduce-scatter.5.cloned.1.call-start = ((), (), s32[]{:S(2)}) async-start(), calls=%async_computation.4 | async-start | bytes 2506752 | tf_op jit(solution)/shard_map/reduce_scatter | solution.py:59
  169.6 2.5 copy-start.1
  172.1 1.9 copy-start.3
  176.6 2.2 copy-start.6
  181.5 12.4 %collective-permute-start = (bf16[1008,192]{1,0:T(8,128)(2,1)S(1)}, bf16[1008,192]{1,0:T(8,128)(2,1)S(1)}, u32[]{:S(2)}, u32[]{:S(2)}) collective-permute-start(bf16[1008,192]{1,0:T(8,128)(2,1)S(1)} %broadcast_select_fusion), channel_id=1, source_target_pairs={{0,1},{1,0},{2,3},{3,2},{4,5},{5,4},{6,7},{7,6},{8,9},{9,8},{10,11... | collective-permute-start | bytes 1161224 | tf_op jit(solution)/shard_map/ppermute | solution.py:76
  194.2 60.5 %copy-start.4 = (s32[96]{0:T(128)S(1)}, s32[96]{0:T(128)}, u32[]{:S(2)}) copy-start(s32[96]{0:T(128)} %param.14) | copy-start | bytes 1156
Sparse Core Ops, SparseCore 0:
  11.8 58.7 all-gather.2
  77.5 42.5 reduce-scatter.6
  122.8 46.7 all-gather.4
  176.8 76.9 reduce-scatter.4
